TPU v7x, 128 devices: a whole 4x4x4 slice. The times are simulated.
128 devices in a mesh: gx: 16 (over x_hi, y, core), gy: 8 (over z, x_lo).
Axes of the slice: x: 4 (x_hi: 2, x_lo: 2; x = x_hi * 2 + x_lo), y: 4, z: 4, core: 2. Of those that a mesh axis runs over, the one named last changes fastest.
Arguments:
- incident: bfloat16 [6, 256, 128, 192], P(None, 'gx', 'gy'), may hold values from -6 to 6
- adjoint_source: bfloat16 [6, 256, 128, 192], P(None, 'gx', 'gy'), may hold values from -6 to 6
- cell_class: int32 [256, 128], P('gx', 'gy'), may hold values from 0 to 7
- slot_table: int32 [8, 8], replicated, may hold values from 0 to 7, each once within a row
- gain_table: float32 [8, 8, 192], replicated, may hold values from 0.3 to 1.5
- admittance: float32 [8, 192], replicated, may hold values from 0.5 to 1.5
- coupling: bfloat16 [8, 192, 192], replicated, may hold values from -0.109375 to 0.109375
- self_inverse: bfloat16 [192, 192], replicated, may hold values from -0.15 to 1.21
Outputs:
- current: bfloat16 [6, 256, 128, 192], P(None, 'gx', 'gy')
- adjoint_state: bfloat16 [6, 256, 128, 192], P(None, 'gx', 'gy')
All inputs are finite; a program needn't handle non-finite values.
Results may differ from a plain program's by a relative error of at most 0.02.
Values may be sent and summed in bfloat16 or wider, within the bound.
A program may use at most 128 MiB of HBM per device.

v0:
```python
import functools

import jax
import jax.numpy as jnp
from jax import lax
from jax.experimental import pallas as pl
from jax.experimental.pallas import tpu as pltpu
from jax.sharding import PartitionSpec as P

MESH = pl.DeviceIdType.MESH
F32 = jnp.float32
BF16 = jnp.bfloat16
SWEEPS = 3
R = 6
N = 16
ROWS = N * N
EDGE = R * N
U = 192
MANY = R * ROWS
T = 128
HALF = 64
STEPS = ((-1, -1), (-1, 0), (-1, 1), (0, -1), (0, 1), (1, -1), (1, 0), (1, 1))
PAIRS = ((0, 5), (1, 6), (2, 7), (3, 4))
TILES = 12
Y_DIRS = ((0, 3, 5), (2, 4, 7))
X_DIRS = ((0, 1, 2), (5, 6, 7))
Y_TILES = ((0, 3, 5, 8, 11), (2, 4, 7, 10, 11))
X_TILES = ((0, 1, 2, 8, 9, 10), (5, 6, 7, 8, 9, 10))


def dot(a, b):
    return jnp.dot(a, b, preferred_element_type=F32)


def dot_nt(a, b):
    return lax.dot_general(a, b, (((1,), (1,)), ((), ())), preferred_element_type=F32)


def iota(shape, dim):
    return lax.broadcasted_iota(jnp.int32, shape, dim)


def low(rows):
    return iota((rows, T), 1) < HALF


def turn(x, shift, axis=0):
    size = x.shape[axis]
    return x if shift % size == 0 else pltpu.roll(x, shift % size, axis)


def spread(tile, corner=None):
    return jnp.concatenate([tile] * R + ([] if corner is None else [corner]), axis=0)


def fold(tile):
    return tile + turn(tile, HALF, 1)


def pack(a, h):
    half = EDGE // 2
    return jnp.concatenate([a, jnp.where(low(half), h[:half], h[half:])], axis=0).astype(BF16)


def unpack(message):
    value = message.astype(F32)
    mixed = value[EDGE:]
    other = turn(mixed, HALF, 1)
    keep = low(EDGE // 2)
    return value[:EDGE], jnp.concatenate([jnp.where(keep, mixed, other), jnp.where(keep, other, mixed)], axis=0)


def kernel(
    nx, ny,
    inc_hbm, src_hbm, cls, slot, gain, adm, coup_hbm, sinv,
    rest_out, back_out, admit_out,
    inc, src, coup, load_sem,
    v0, vm, vp, adj, near_a, near_h, far_a, far_h, gains, lhs, weights, weights_t, partial,
    admit, admit_e, inc_e, src_e, gains_y, gains_x, solve, solve_t, corner_s,
    send_y, send_x, send_c, recv_y, recv_x, recv_c,
    send_sem, recv_sem,
):
    gx, gy = lax.axis_index("gx"), lax.axis_index("gy")
    left, right = lax.rem(gx + nx - 1, nx), lax.rem(gx + 1, nx)
    down, up = lax.rem(gy + ny - 1, ny), lax.rem(gy + 1, ny)
    y_to = ((gx, down), (gx, up))
    x_to = ((left, gy), (right, gy))
    c_to = ((left, down), (right, down), (left, up), (right, up))

    barrier = pltpu.get_barrier_semaphore()
    for where in y_to + x_to + c_to:
        pl.semaphore_signal(barrier, inc=1, device_id=where, device_id_type=MESH)

    loads = [
        pltpu.make_async_copy(a, b, load_sem.at[k])
        for k, (a, b) in enumerate(((inc_hbm, inc), (coup_hbm, coup), (src_hbm, src)))
    ]
    stores = [
        pltpu.make_async_copy(a, b, load_sem.at[3 + k])
        for k, (a, b) in enumerate(((inc, rest_out), (src, back_out), (admit, admit_out)))
    ]
    for load in loads:
        load.start()

    def take(ref):
        parts = [ref[pl.ds(e * (N - 1), EDGE, stride=N), :] for e in range(2)]
        for e in range(2):
            for r in range(R):
                start = r * ROWS + e * (ROWS - N)
                parts.append(ref[start:start + N, :])
        return jnp.concatenate(parts, axis=0)

    def edge_rows(data, a_ref, h_ref, e_ref):
        h_ref[...] = jnp.zeros_like(h_ref)
        for r in range(R):
            a_ref[r * ROWS:(r + 1) * ROWS, :] = data[r * ROWS:(r + 1) * ROWS, 0:T].astype(F32)
            h_ref[r * ROWS:(r + 1) * ROWS, 0:HALF] = data[r * ROWS:(r + 1) * ROWS, T:U].astype(F32)
        for k, ref in enumerate((a_ref, h_ref)):
            columns = slice(k * T, (k + 1) * T)
            e_ref[:, columns] = take(ref)
            ref[...] = jnp.zeros_like(ref)

    def scale_e():
        return jnp.concatenate([spread(admit_e[e * N:(e + 1) * N, :]) for e in range(4)], axis=0)

    def corners(k, value):
        corner_s[k, 0:EDGE, :] = value
        return jnp.concatenate([corner_s[k, pl.ds(0, 8, stride=N), :], corner_s[k, pl.ds(N - 1, 8, stride=N), :]], axis=0)

    def edges_f(v):
        near_e = jnp.concatenate([take(near_a), take(near_h)], axis=1)
        rest = (inc_e[...] - near_e).astype(BF16)
        cur_e = dot(rest[:, 0:U], solve[...]) * scale_e()
        for e in range(2):
            rows = slice(e * EDGE, (e + 1) * EDGE)
            send_y[0, v, e] = pack(cur_e[rows, 0:T], cur_e[rows, T:])
            both = jnp.concatenate([corners(2 * e, cur_e[rows, 0:T]), corners(2 * e + 1, cur_e[rows, T:])], axis=1)
            send_c[0, v, 2 * e] = both[0:8]
            send_c[0, v, 2 * e + 1] = both[8:16]
        for e in range(2):
            rows = slice((2 + e) * EDGE, (3 + e) * EDGE)
            send_x[0, v, e] = pack(cur_e[rows, 0:T], cur_e[rows, T:])

    def edges_a(v):
        far_e = jnp.concatenate([take(far_a), take(far_h)], axis=1)
        back = ((src_e[...] - far_e) * scale_e()).astype(BF16)
        adj_e = dot(back[:, 0:U], solve_t[...])
        for e in range(2):
            rows = slice(e * EDGE, (e + 1) * EDGE)
            cut = [corners(4 + 2 * e + k, adj_e[rows, k * T:(k + 1) * T]) for k in range(2)]
            state = jnp.concatenate([adj_e[rows], jnp.concatenate(cut, axis=1)], axis=0).astype(BF16)
            out = []
            for k, t in enumerate(Y_TILES[e]):
                gain_k = gains_y[e, :, k * T:(k + 1) * T]
                out.append(dot(state, weights_t[:, t * T:(t + 1) * T]) * spread(gain_k[0:N], gain_k[N:]))
            part_a = turn(out[0][:EDGE], -1) + out[1][:EDGE] + turn(out[2][:EDGE], 1)
            part_h = fold(
                jnp.where(low(EDGE), turn(out[3][:EDGE], -1), turn(out[3][:EDGE], 1)) + out[4][:EDGE]
            )
            tail_a = out[0][EDGE:] + out[1][EDGE:] + out[2][EDGE:]
            tail_h = fold(out[3][EDGE:] + out[4][EDGE:])
            send_y[1, v, e] = pack(part_a, part_h)
            tail = jnp.concatenate([tail_a, tail_h], axis=1)
            send_c[1, v, 2 * e] = tail[0:8]
            send_c[1, v, 2 * e + 1] = tail[8:16]
        for e in range(2):
            state = adj_e[(2 + e) * EDGE:(3 + e) * EDGE].astype(BF16)
            out = []
            for k, t in enumerate(X_TILES[e]):
                out.append(dot(state, weights_t[:, t * T:(t + 1) * T]) * spread(gains_x[e, :, k * T:(k + 1) * T]))
            part_a = turn(out[0], -1) + out[1] + turn(out[2], 1)
            part_h = fold(turn(out[3], -1) + out[4] + turn(out[5], 1))
            send_x[1, v, e] = pack(part_a, part_h)

    inside_y = (gy > 0, gy < ny - 1)
    inside_x = (gx > 0, gx < nx - 1)

    def copies(kind, v):
        made = []
        for e in range(2):
            made.append((send_y.at[kind, v, e], recv_y.at[kind, v, 1 - e], y_to[e], e, 1 - e, inside_y[e], inside_y[1 - e]))
        for e in range(2):
            made.append((send_x.at[kind, v, e], recv_x.at[kind, v, 1 - e], x_to[e], 2 + e, 3 - e, inside_x[e], inside_x[1 - e]))
        for q in range(4):
            goes = inside_y[q // 2] & inside_x[q % 2]
            comes = inside_y[1 - q // 2] & inside_x[1 - q % 2]
            made.append((send_c.at[kind, v, q], recv_c.at[kind, v, 3 - q], c_to[q], 4 + q, 7 - q, goes, comes))
        return [
            (
                pltpu.make_async_remote_copy(
                    src_ref=a, dst_ref=b, send_sem=send_sem.at[kind, v, s], recv_sem=recv_sem.at[kind, v, t],
                    device_id=where, device_id_type=MESH,
                ),
                goes,
                comes,
            )
            for a, b, where, s, t, goes, comes in made
        ]

    def start(kind, v):
        for copy, goes, _ in copies(kind, v):
            pl.when(goes)(copy.start)

    def arrive(kind, v):
        for copy, _, comes in copies(kind, v):
            pl.when(comes)(copy.wait_recv)

    def sent(kind, v):
        for copy, goes, _ in copies(kind, v):
            pl.when(goes)(copy.wait_send)

    def no_sender():
        def clear(ref, q):
            for kind in range(2):
                for v in range(SWEEPS):
                    ref[kind, v, q] = jnp.zeros(ref.shape[3:], ref.dtype)

        for e in range(2):
            pl.when(jnp.logical_not(inside_y[e]))(functools.partial(clear, recv_y, e))
            pl.when(jnp.logical_not(inside_x[e]))(functools.partial(clear, recv_x, e))
        for q in range(4):
            pl.when(jnp.logical_not(inside_y[q // 2] & inside_x[q % 2]))(functools.partial(clear, recv_c, q))

    def right_f():
        near = jnp.concatenate([near_a[0:MANY, :], near_h[0:MANY, 0:HALF]], axis=1)
        return (inc[...].astype(F32) - near).astype(BF16)

    def right_a():
        far = jnp.concatenate([far_a[0:MANY, :], far_h[0:MANY, 0:HALF]], axis=1)
        back = src[...].astype(F32) - far
        back = [back[r * ROWS:(r + 1) * ROWS] * admit[:, 0:U] for r in range(R)]
        return jnp.concatenate(back, axis=0).astype(BF16)

    shifted = {-1: vm, 0: v0, 1: vp}

    def main_f():
        cur = dot(right_f(), solve[...])
        for r in range(R):
            one_cur = cur[r * ROWS:(r + 1) * ROWS] * admit[...]
            v0[r, N:N + ROWS, :] = one_cur.astype(BF16)
            vm[r, N:N + ROWS, :] = turn(one_cur, 1).astype(BF16)
            vp[r, N:N + ROWS, :] = turn(one_cur, -1).astype(BF16)
        for r in range(R):
            rows = slice(r * ROWS, (r + 1) * ROWS)

            def nearby(d, columns):
                sx, sy = STEPS[d]
                return shifted[sy][r, N * (1 + sx):N * (1 + sx) + ROWS, columns]

            for d in range(8):
                columns = slice(d * T, (d + 1) * T)
                lhs[rows, columns] = nearby(d, slice(0, T)) * gains[:, columns]
            for p, (d0, d1) in enumerate(PAIRS):
                columns = slice((8 + p) * T, (9 + p) * T)
                both = jnp.where(low(ROWS), nearby(d0, slice(T, 2 * T)), nearby(d1, slice(T, 2 * T)))
                lhs[rows, columns] = both * gains[:, columns]
        near = dot(lhs[...], weights[...])
        near_a[0:MANY, :] = near[:, 0:T]
        near_h[0:MANY, :] = near[:, T:]

    def main_a():
        adj[...] = dot(right_a(), solve_t[...]).astype(BF16)
        for t in range(TILES // 2):
            columns = slice(2 * t * T, 2 * (t + 1) * T)
            value = dot(adj[...], weights_t[:, columns]).astype(BF16)
            for r in range(R):
                partial[r, N:N + ROWS, columns] = value[r * ROWS:(r + 1) * ROWS] * gains[:, columns]
        for r in range(R):

            def part(x, t):
                return partial[r, x * N:(x + 1) * N, t * T:(t + 1) * T].astype(F32)

            for x in range(N):
                sums = {sy: None for sy in (-1, 0, 1)}
                for d, (sx, sy) in enumerate(STEPS):
                    value = part(1 + x - sx, d)
                    sums[sy] = value if sums[sy] is None else sums[sy] + value
                a = turn(sums[1], 1) + sums[0] + turn(sums[-1], -1)
                tops = {sy: jnp.where(low(N), part(2 + x, 9 + sy), part(x, 9 + sy)) for sy in (-1, 0, 1)}
                mid = part(1 + x, 11)
                below = tops[-1] + jnp.where(low(N), mid, 0.0)
                above = tops[1] + jnp.where(low(N), 0.0, mid)
                h = fold(turn(above, 1) + tops[0] + turn(below, -1))
                at = r * ROWS + x * N
                far_a[at:at + N, :] = a
                far_h[at:at + N, :] = h

    def add_y(e, ref, value, tail):
        y0 = e * (N - 1)
        for at, piece in (
            (pl.ds(y0, EDGE, stride=N), value),
            (pl.ds(y0, 8, stride=ROWS), tail[0:8]),
            (pl.ds(y0 + ROWS - N, 8, stride=ROWS), tail[8:16]),
        ):
            ref[at, :] = ref[at, :] + piece

    def add_x(e, ref, value):
        for r in range(R):
            at = r * ROWS + e * (ROWS - N)
            ref[at:at + N, :] = ref[at:at + N, :] + value[r * N:(r + 1) * N]

    def correct_f(v):
        for e in range(2):
            a, h = unpack(recv_y[0, v, e])
            tail = jnp.concatenate([recv_c[0, v, 2 * e], recv_c[0, v, 2 * e + 1]], axis=0)
            tail_a, tail_h = tail[:, 0:T], tail[:, T:]
            tiles = [
                (turn(a, 1), tail_a), (a, tail_a), (turn(a, -1), tail_a),
                (jnp.where(low(EDGE), turn(h, 1), turn(h, -1)), tail_h), (h, tail_h),
            ]
            scaled = []
            for k, tile in enumerate(tiles):
                gain_k = gains_y[e, :, k * T:(k + 1) * T]
                scaled.append((jnp.concatenate(tile, axis=0) * spread(gain_k[0:N], gain_k[N:])).astype(BF16))
            matrix = jnp.concatenate([weights[t * T:(t + 1) * T, :] for t in Y_TILES[e]], axis=0)
            extra = dot(jnp.concatenate(scaled, axis=1), matrix)
            add_y(e, near_a, extra[:EDGE, 0:T], extra[EDGE:, 0:T])
            add_y(e, near_h, extra[:EDGE, T:], extra[EDGE:, T:])
        for e in range(2):
            a, h = unpack(recv_x[0, v, e])
            tiles = [turn(a, 1), a, turn(a, -1), turn(h, 1), h, turn(h, -1)]
            scaled = []
            for k, tile in enumerate(tiles):
                scaled.append((tile * spread(gains_x[e, :, k * T:(k + 1) * T])).astype(BF16))
            matrix = jnp.concatenate([weights[t * T:(t + 1) * T, :] for t in X_TILES[e]], axis=0)
            extra = dot(jnp.concatenate(scaled, axis=1), matrix)
            add_x(e, near_a, extra[:, 0:T])
            add_x(e, near_h, extra[:, T:])

    def correct_a(v):
        for e in range(2):
            a, h = unpack(recv_y[1, v, e])
            tail = jnp.concatenate([recv_c[1, v, 2 * e], recv_c[1, v, 2 * e + 1]], axis=0)
            add_y(e, far_a, a, tail[:, 0:T])
            add_y(e, far_h, h, tail[:, T:])
        for e in range(2):
            a, h = unpack(recv_x[1, v, e])
            add_x(e, far_a, a)
            add_x(e, far_h, h)

    one = jnp.float32(1.0)
    has_left, has_right = jnp.where(gx > 0, 1.0, 0.0) * one, jnp.where(gx < nx - 1, 1.0, 0.0) * one
    has_down, has_up = jnp.where(gy > 0, 1.0, 0.0) * one, jnp.where(gy < ny - 1, 1.0, 0.0) * one

    def chooser(rows, columns, wanted):
        return jnp.where(iota((rows, columns), 0) == wanted, 1.0, 0.0).astype(BF16)

    lane = iota((U, 2 * T), 1)
    dup = chooser(U, 2 * T, jnp.where(lane < U, lane, lane - HALF))
    dup_back = chooser(U, 2 * T, jnp.where(lane < HALF, lane + T, jnp.where(lane < T, lane + HALF, lane - T)))
    eye = chooser(U, U, iota((U, U), 1))
    solve[...] = dot(sinv[...], dup).astype(BF16)
    solve_n = dot_nt(eye, sinv[...]).astype(BF16)
    solve_t[...] = dot(solve_n, dup_back).astype(BF16)

    adm_high = adm[...].astype(BF16).astype(F32)
    adm_both = jnp.concatenate([adm_high, adm[...] - adm_high], axis=0).astype(BF16)
    adm_table = dot(adm_both, dup).astype(BF16)

    diag = iota((N, N), 0) == iota((N, N), 1)
    spots = [jnp.where(diag, cls[x:x + 1, :].astype(F32), 0.0) for x in range(N)]
    kind = dot(jnp.concatenate(spots, axis=0).astype(BF16), jnp.ones((N, N), BF16))

    def onehot(kinds):
        which = lax.rem(iota((kinds.shape[0], N), 1), 8)
        return jnp.where(which.astype(F32) == kinds, 1.0, 0.0).astype(BF16)

    kind_e = jnp.concatenate(
        [
            jnp.broadcast_to(cls[:, 0:1].astype(F32), (N, N)),
            jnp.broadcast_to(cls[:, N - 1:N].astype(F32), (N, N)),
            kind[0:N],
            kind[ROWS - N:ROWS],
        ],
        axis=0,
    )
    hot, hot_e = onehot(kind), onehot(kind_e)
    admit_e[...] = dot(hot_e, adm_table)
    corner_s[...] = jnp.zeros_like(corner_s)
    no_sender()
    loads[0].wait()
    edge_rows(inc, near_a, near_h, inc_e)
    pick = [
        jnp.where(iota((8, 64), 1) == iota((8, 64), 0) * 8 + slot[:, d:d + 1], 1.0, 0.0)
        for d in range(8)
    ]
    pick = jnp.concatenate(pick, axis=0).astype(BF16)
    gain_dup = dot(gain[...].astype(BF16), dup).astype(BF16)
    table64 = dot(pick, gain_dup)
    pieces = [table64[d * 8:(d + 1) * 8, 0:T] for d in range(8)]
    for d0, d1 in PAIRS:
        pieces.append(jnp.where(low(8), table64[d0 * 8:(d0 + 1) * 8, T:], table64[d1 * 8:(d1 + 1) * 8, T:]))
    table = jnp.concatenate(pieces, axis=1)
    table = jnp.concatenate([table, jnp.zeros_like(table)], axis=0).astype(BF16)
    edge_gain = dot(hot_e, table)
    spot = iota((N, T), 0)

    def along(j):
        return jnp.where((spot + j >= 0) & (spot + j < N), 1.0, 0.0)

    lows = jnp.where(low(N), 1.0, 0.0)
    for e, exists in enumerate((has_down, has_up)):
        raw = edge_gain[e * N:(e + 1) * N]
        first = jnp.where(spot < 8, 1.0, 0.0)
        side = first * has_left + (1.0 - first) * has_right
        for k, t in enumerate(Y_TILES[e]):
            tile = raw[:, t * T:(t + 1) * T]
            ends = jnp.where(spot < 8, jnp.broadcast_to(tile[0:1], (N, T)), jnp.broadcast_to(tile[N - 1:N], (N, T)))
            if k < 3:
                keep = along(k - 1)
                corner = (first, 0.0 * first, 1.0 - first)[k]
            elif k == 3:
                keep = lows * along(-1) + (1.0 - lows) * along(1)
                corner = lows * first + (1.0 - lows) * (1.0 - first)
            else:
                keep = lows if e == 0 else 1.0 - lows
                corner = 0.0 * first
            gains_y[e, 0:N, k * T:(k + 1) * T] = tile * keep * exists
            gains_y[e, N:2 * N, k * T:(k + 1) * T] = ends * corner * side * exists
    for e, exists in enumerate((has_left, has_right)):
        raw = edge_gain[(2 + e) * N:(3 + e) * N]
        for k, t in enumerate(X_TILES[e]):
            keep = along(k % 3 - 1)
            if k >= 3:
                keep = keep * (lows if e == 0 else 1.0 - lows)
            gains_x[e, :, k * T:(k + 1) * T] = raw[:, t * T:(t + 1) * T] * keep * exists

    loads[1].wait()
    weights[...] = jnp.zeros_like(weights)
    for d in range(8):
        weights[d * T:(d + 1) * T, 0:U] = coup[d, 0:T, :]
    for p, (d0, d1) in enumerate(PAIRS):
        base = (8 + p) * T
        weights[base:base + HALF, 0:U] = coup[d0, T:U, :]
        weights[base + HALF:base + T, 0:U] = coup[d1, T:U, :]
    row = iota((2 * T, U), 0)
    place = jnp.where(row < HALF, -1, jnp.where(row < T, row + HALF, row - T))
    order = jnp.where(iota((2 * T, U), 1) == place, 1.0, 0.0).astype(BF16)
    for t in range(TILES):
        weights_t[:, t * T:(t + 1) * T] = dot_nt(order, weights[t * T:(t + 1) * T, 0:U]).astype(BF16)

    loads[2].wait()
    edge_rows(src, far_a, far_h, src_e)

    admit[...] = dot(hot, adm_table)
    stores[2].start()

    def inside(rows, sx, sy):
        r = iota((rows, T), 0)
        x, y = r // N + sx, lax.rem(r, N) + sy
        return (x >= 0) & (x < N) & (y >= 0) & (y < N)

    for t in range(TILES):
        value = dot(hot, table[:, t * T:(t + 1) * T])
        if t < 8:
            keep = jnp.where(inside(ROWS, *STEPS[t]), 1.0, 0.0)
        else:
            d0, d1 = PAIRS[t - 8]
            keep = jnp.where(
                low(ROWS), jnp.where(inside(ROWS, *STEPS[d0]), 1.0, 0.0), jnp.where(inside(ROWS, *STEPS[d1]), 1.0, 0.0)
            )
        gains[:, t * T:(t + 1) * T] = (value * keep).astype(BF16)

    for ref in (v0, vm, vp):
        for r in range(R):
            ref[r, 0:N, :] = jnp.zeros((N, 2 * T), BF16)
            ref[r, (N + 1) * N:(N + 2) * N, :] = jnp.zeros((N, 2 * T), BF16)
    for r in range(R):
        partial[r, 0:N, :] = jnp.zeros((N, TILES * T), BF16)
        partial[r, (N + 1) * N:(N + 2) * N, :] = jnp.zeros((N, TILES * T), BF16)

    edges_f(0)
    edges_a(0)
    pl.semaphore_wait(barrier, 8)
    start(0, 0)
    start(1, 0)
    main_f()

    def sweep(v, carry):
        main_a()
        arrive(0, v)
        correct_f(v)
        edges_f(v + 1)
        start(0, v + 1)
        main_f()
        arrive(1, v)
        correct_a(v)
        edges_a(v + 1)
        start(1, v + 1)
        return carry

    lax.fori_loop(0, SWEEPS - 1, sweep, 0)
    main_a()
    arrive(0, SWEEPS - 1)
    correct_f(SWEEPS - 1)
    inc[...] = right_f()
    stores[0].start()
    arrive(1, SWEEPS - 1)
    correct_a(SWEEPS - 1)
    src[...] = right_a()
    stores[1].start()
    for kind in range(2):
        for v in range(SWEEPS):
            sent(kind, v)
    for store in stores:
        store.wait()


def last(rest, back, admit, sinv, cur_out, adj_out):
    cur = dot(rest[...], sinv[...])
    for r in range(R // 2):
        rows = slice(r * ROWS, (r + 1) * ROWS)
        cur_out[rows, :] = (cur[rows] * admit[:, 0:U]).astype(BF16)
    adj_out[...] = dot_nt(back[...], sinv[...]).astype(BF16)


def solution(mesh):
    nx, ny = mesh.shape["gx"], mesh.shape["gy"]

    def local(inc, src, cls, slot, gain, adm, coup, sinv):
        vmem = pl.BlockSpec(memory_space=pltpu.VMEM)
        anywhere = pl.BlockSpec(memory_space=pl.ANY)
        out = jax.ShapeDtypeStruct((R * ROWS, U), BF16)
        rest, back, admit = pl.pallas_call(
            functools.partial(kernel, nx, ny),
            out_shape=(out, out, jax.ShapeDtypeStruct((ROWS, 2 * T), F32)),
            in_specs=[anywhere, anywhere, vmem, vmem, vmem, vmem, anywhere, vmem],
            out_specs=(anywhere, anywhere, anywhere),
            scratch_shapes=[
                pltpu.VMEM((R * ROWS, U), BF16),
                pltpu.VMEM((R * ROWS, U), BF16),
                pltpu.VMEM((8, U, U), BF16),
                pltpu.SemaphoreType.DMA((6,)),
                pltpu.VMEM((R, ROWS + 2 * N, 2 * T), BF16),
                pltpu.VMEM((R, ROWS + 2 * N, 2 * T), BF16),
                pltpu.VMEM((R, ROWS + 2 * N, 2 * T), BF16),
                pltpu.VMEM((R * ROWS, 2 * T), BF16),
                pltpu.VMEM((8 * ROWS, T), F32),
                pltpu.VMEM((8 * ROWS, T), F32),
                pltpu.VMEM((8 * ROWS, T), F32),
                pltpu.VMEM((8 * ROWS, T), F32),
                pltpu.VMEM((ROWS, TILES * T), BF16),
                pltpu.VMEM((R * ROWS, TILES * T), BF16),
                pltpu.VMEM((TILES * T, 2 * T), BF16),
                pltpu.VMEM((2 * T, TILES * T), BF16),
                pltpu.VMEM((R, ROWS + 2 * N, TILES * T), BF16),
                pltpu.VMEM((ROWS, 2 * T), F32),
                pltpu.VMEM((4 * N, 2 * T), F32),
                pltpu.VMEM((4 * EDGE, 2 * T), F32),
                pltpu.VMEM((4 * EDGE, 2 * T), F32),
                pltpu.VMEM((2, 2 * N, 5 * T), F32),
                pltpu.VMEM((2, N, 6 * T), F32),
                pltpu.VMEM((U, 2 * T), BF16),
                pltpu.VMEM((U, 2 * T), BF16),
                pltpu.VMEM((8, 8 * N, T), F32),
                pltpu.VMEM((2, SWEEPS, 2, EDGE + EDGE // 2, T), BF16),
                pltpu.VMEM((2, SWEEPS, 2, EDGE + EDGE // 2, T), BF16),
                pltpu.VMEM((2, SWEEPS, 4, 8, 2 * T), F32),
                pltpu.VMEM((2, SWEEPS, 2, EDGE + EDGE // 2, T), BF16),
                pltpu.VMEM((2, SWEEPS, 2, EDGE + EDGE // 2, T), BF16),
                pltpu.VMEM((2, SWEEPS, 4, 8, 2 * T), F32),
                pltpu.SemaphoreType.DMA((2, SWEEPS, 8)),
                pltpu.SemaphoreType.DMA((2, SWEEPS, 8)),
            ],
            compiler_params=pltpu.CompilerParams(
                collective_id=0, has_side_effects=True, vmem_limit_bytes=60 * 1024 * 1024
            ),
        )(
            inc.reshape(R * ROWS, U), src.reshape(R * ROWS, U), cls, slot, gain.reshape(64, U), adm, coup, sinv
        )
        half = pl.BlockSpec((R * ROWS // 2, U), lambda i: (i, 0))
        cur, adj = pl.pallas_call(
            last,
            grid=(2,),
            out_shape=(out, out),
            in_specs=[half, half, pl.BlockSpec((ROWS, 2 * T), lambda i: (0, 0)), pl.BlockSpec((U, U), lambda i: (0, 0))],
            out_specs=(half, half),
        )(rest, back, admit, sinv)
        return cur.reshape(R, N, N, U), adj.reshape(R, N, N, U)

    placed = (P(None, "gx", "gy", None), P(None, "gx", "gy", None), P("gx", "gy"), P(), P(), P(), P(), P())
    return jax.shard_map(
        local, mesh=mesh, in_specs=placed, out_specs=(placed[0], placed[0]), check_vma=False
    )
```

profile of v0, /device:TPU:0, one launch (start us, length us, event | category | flops | bytes accessed | tf_op | source)
XLA Modules:
  0.0 38.1 jit_solution(1727275779140989008)
XLA Ops:
  0.6 34.6 %shard_map.95 = (bf16[1536,192]{1,0:T(8,128)(2,1)}, bf16[1536,192]{1,0:T(8,128)(2,1)}, f32[256,256]{1,0:T(8,128)}) custom-call(bf16[1536,192]{1,0:T(8,128)(2,1)} %bitcast.5, bf16[1536,192]{1,0:T(8,128)(2,1)} %bitcast.6, s32[16,16]{1,0:T(8,128)} %cls.1, s32[8,8]{1,0:T(8,128)} %slot.1, f32[64,192]{1,0:T(8,128)} %bitcast.7, f32[8,192]{1,0:T(8,128)} %adm.1, ...), custom_call_target="tpu_custom_call" | custom-call | tf_op jit(solution)/shard_map/pallas_call | solution.py:524
  35.3 2.9 %shard_map.96 = (bf16[1536,192]{1,0:T(8,128)(2,1)}, bf16[1536,192]{1,0:T(8,128)(2,1)}) custom-call(bf16[1536,192]{1,0:T(8,128)(2,1)} %get-tuple-element.7.rest, bf16[1536,192]{1,0:T(8,128)(2,1)} %get-tuple-element.8.back, f32[256,256]{1,0:T(8,128)} %get-tuple-element.9.admit, bf16[192,192]{1,0:T(8,128)(2,1)} %sinv.3), custom_call_target="tpu_custom_call" | custom-call | tf_op jit(solution)/shard_map/pallas_call | solution.py:572
where the time goes:
time: 38.3 us; the launch traced here: 38.1 us
  Pallas kernels  37.5 us (98%)
  between operations  0.64 us (2%)
    pallas_call x1, Pallas kernels, local(): pl.pallas_call(functools.partial(kernel, nx, ny), out_shape=(out, out, ja...  34.6 us
    pallas_call x1, Pallas kernels, local(): pl.pallas_call(last, grid=(2,), out_shape=(out, out), in_specs=[half, hal...  2.86 us

commit v1 on v0

--- a/solution.py
+++ b/solution.py
@@ -489,7 +489,8 @@
         start(1, v + 1)
         return carry
 
-    lax.fori_loop(0, SWEEPS - 1, sweep, 0)
+    for v in range(SWEEPS - 1):
+        sweep(v, 0)
     main_a()
     arrive(0, SWEEPS - 1)
     correct_f(SWEEPS - 1)

time: 38.3 us -> 37.1 us (0.969)
  Pallas kernels: 37.5 us -> 36.1 us
    pallas_call x1, Pallas kernels: 34.6 us -> 33.2 us  [local(): pl.pallas_call(functools.partial(kernel, nx, ny), out_shape=(out, out, ja...]
where the time goes in v1:
time: 37.1 us; the launch traced here: 36.7 us
  Pallas kernels  36.1 us (97%)
  between operations  0.64 us (2%)
    pallas_call x1, Pallas kernels, local(): pl.pallas_call(functools.partial(kernel, nx, ny), out_shape=(out, out, ja...  33.2 us
    pallas_call x1, Pallas kernels, local(): pl.pallas_call(last, grid=(2,), out_shape=(out, out), in_specs=[half, hal...  2.86 us

profile of v1, /device:TPU:0, one launch (start us, length us, event | category | flops | bytes accessed | tf_op | source)
XLA Modules:
  0.0 36.7 jit_solution(15815296319911913199)
XLA Ops:
  0.6 33.2 %shard_map.95 = (bf16[1536,192]{1,0:T(8,128)(2,1)}, bf16[1536,192]{1,0:T(8,128)(2,1)}, f32[256,256]{1,0:T(8,128)}) custom-call(bf16[1536,192]{1,0:T(8,128)(2,1)} %bitcast.5, bf16[1536,192]{1,0:T(8,128)(2,1)} %bitcast.6, s32[16,16]{1,0:T(8,128)} %cls.1, s32[8,8]{1,0:T(8,128)} %slot.1, f32[64,192]{1,0:T(8,128)} %bitcast.7, f32[8,192]{1,0:T(8,128)} %adm.1, ...), custom_call_target="tpu_custom_call" | custom-call | tf_op jit(solution)/shard_map/pallas_call | solution.py:525
  33.9 2.9 %shard_map.96 = (bf16[1536,192]{1,0:T(8,128)(2,1)}, bf16[1536,192]{1,0:T(8,128)(2,1)}) custom-call(bf16[1536,192]{1,0:T(8,128)(2,1)} %get-tuple-element.7.rest, bf16[1536,192]{1,0:T(8,128)(2,1)} %get-tuple-element.8.back, f32[256,256]{1,0:T(8,128)} %get-tuple-element.9.admit, bf16[192,192]{1,0:T(8,128)(2,1)} %sinv.3), custom_call_target="tpu_custom_call" | custom-call | tf_op jit(solution)/shard_map/pallas_call | solution.py:573

commit v2 on v1

--- a/solution.py
+++ b/solution.py
@@ -74,7 +74,7 @@
     nx, ny,
     inc_hbm, src_hbm, cls, slot, gain, adm, coup_hbm, sinv,
     rest_out, back_out, admit_out,
-    inc, src, coup, load_sem,
+    inc, src, coup, load_sem, gains_w,
     v0, vm, vp, adj, near_a, near_h, far_a, far_h, gains, lhs, weights, weights_t, partial,
     admit, admit_e, inc_e, src_e, gains_y, gains_x, solve, solve_t, corner_s,
     send_y, send_x, send_c, recv_y, recv_x, recv_c,
@@ -141,6 +141,14 @@
             rows = slice((2 + e) * EDGE, (3 + e) * EDGE)
             send_x[0, v, e] = pack(cur_e[rows, 0:T], cur_e[rows, T:])
 
+    def products(state, tiles):
+        out = []
+        for k in range(0, len(tiles), 2):
+            two = tiles[k:k + 2]
+            value = dot(state, jnp.concatenate([weights_t[:, t * T:(t + 1) * T] for t in two], axis=1))
+            out += [value[:, i * T:(i + 1) * T] for i in range(len(two))]
+        return out
+
     def edges_a(v):
         far_e = jnp.concatenate([take(far_a), take(far_h)], axis=1)
         back = ((src_e[...] - far_e) * scale_e()).astype(BF16)
@@ -150,9 +158,9 @@
             cut = [corners(4 + 2 * e + k, adj_e[rows, k * T:(k + 1) * T]) for k in range(2)]
             state = jnp.concatenate([adj_e[rows], jnp.concatenate(cut, axis=1)], axis=0).astype(BF16)
             out = []
-            for k, t in enumerate(Y_TILES[e]):
+            for k, value in enumerate(products(state, Y_TILES[e])):
                 gain_k = gains_y[e, :, k * T:(k + 1) * T]
-                out.append(dot(state, weights_t[:, t * T:(t + 1) * T]) * spread(gain_k[0:N], gain_k[N:]))
+                out.append(value * spread(gain_k[0:N], gain_k[N:]))
             part_a = turn(out[0][:EDGE], -1) + out[1][:EDGE] + turn(out[2][:EDGE], 1)
             part_h = fold(
                 jnp.where(low(EDGE), turn(out[3][:EDGE], -1), turn(out[3][:EDGE], 1)) + out[4][:EDGE]
@@ -166,8 +174,8 @@
         for e in range(2):
             state = adj_e[(2 + e) * EDGE:(3 + e) * EDGE].astype(BF16)
             out = []
-            for k, t in enumerate(X_TILES[e]):
-                out.append(dot(state, weights_t[:, t * T:(t + 1) * T]) * spread(gains_x[e, :, k * T:(k + 1) * T]))
+            for k, value in enumerate(products(state, X_TILES[e])):
+                out.append(value * spread(gains_x[e, :, k * T:(k + 1) * T]))
             part_a = turn(out[0], -1) + out[1] + turn(out[2], 1)
             part_h = fold(turn(out[3], -1) + out[4] + turn(out[5], 1))
             send_x[1, v, e] = pack(part_a, part_h)
@@ -233,8 +241,11 @@
 
     shifted = {-1: vm, 0: v0, 1: vp}
 
+    halves = (slice(0, MANY // 2), slice(MANY // 2, MANY))
+
     def main_f():
-        cur = dot(right_f(), solve[...])
+        rest = right_f()
+        cur = jnp.concatenate([dot(rest[rows], solve[...]) for rows in halves], axis=0)
         for r in range(R):
             one_cur = cur[r * ROWS:(r + 1) * ROWS] * admit[...]
             v0[r, N:N + ROWS, :] = one_cur.astype(BF16)
@@ -254,21 +265,24 @@
                 columns = slice((8 + p) * T, (9 + p) * T)
                 both = jnp.where(low(ROWS), nearby(d0, slice(T, 2 * T)), nearby(d1, slice(T, 2 * T)))
                 lhs[rows, columns] = both * gains[:, columns]
-        near = dot(lhs[...], weights[...])
-        near_a[0:MANY, :] = near[:, 0:T]
-        near_h[0:MANY, :] = near[:, T:]
+        for rows in halves:
+            near = dot(lhs[rows, :], weights[...])
+            near_a[rows, :] = near[:, 0:T]
+            near_h[rows, :] = near[:, T:]
 
     def main_a():
-        adj[...] = dot(right_a(), solve_t[...]).astype(BF16)
+        back = right_a()
+        for rows in halves:
+            adj[rows, :] = dot(back[rows], solve_t[...]).astype(BF16)
         for t in range(TILES // 2):
             columns = slice(2 * t * T, 2 * (t + 1) * T)
-            value = dot(adj[...], weights_t[:, columns]).astype(BF16)
+            value = dot(adj[...], weights_t[:, columns])
             for r in range(R):
-                partial[r, N:N + ROWS, columns] = value[r * ROWS:(r + 1) * ROWS] * gains[:, columns]
+                partial[r, N:N + ROWS, columns] = value[r * ROWS:(r + 1) * ROWS] * gains_w[:, columns]
         for r in range(R):
 
             def part(x, t):
-                return partial[r, x * N:(x + 1) * N, t * T:(t + 1) * T].astype(F32)
+                return partial[r, x * N:(x + 1) * N, t * T:(t + 1) * T]
 
             for x in range(N):
                 sums = {sy: None for sy in (-1, 0, 1)}
@@ -460,14 +474,15 @@
                 low(ROWS), jnp.where(inside(ROWS, *STEPS[d0]), 1.0, 0.0), jnp.where(inside(ROWS, *STEPS[d1]), 1.0, 0.0)
             )
         gains[:, t * T:(t + 1) * T] = (value * keep).astype(BF16)
+        gains_w[:, t * T:(t + 1) * T] = value * keep
 
     for ref in (v0, vm, vp):
         for r in range(R):
             ref[r, 0:N, :] = jnp.zeros((N, 2 * T), BF16)
             ref[r, (N + 1) * N:(N + 2) * N, :] = jnp.zeros((N, 2 * T), BF16)
     for r in range(R):
-        partial[r, 0:N, :] = jnp.zeros((N, TILES * T), BF16)
-        partial[r, (N + 1) * N:(N + 2) * N, :] = jnp.zeros((N, TILES * T), BF16)
+        partial[r, 0:N, :] = jnp.zeros((N, TILES * T), F32)
+        partial[r, (N + 1) * N:(N + 2) * N, :] = jnp.zeros((N, TILES * T), F32)
 
     edges_f(0)
     edges_a(0)
@@ -532,6 +547,7 @@
                 pltpu.VMEM((R * ROWS, U), BF16),
                 pltpu.VMEM((8, U, U), BF16),
                 pltpu.SemaphoreType.DMA((6,)),
+                pltpu.VMEM((ROWS, TILES * T), F32),
                 pltpu.VMEM((R, ROWS + 2 * N, 2 * T), BF16),
                 pltpu.VMEM((R, ROWS + 2 * N, 2 * T), BF16),
                 pltpu.VMEM((R, ROWS + 2 * N, 2 * T), BF16),
@@ -544,7 +560,7 @@
                 pltpu.VMEM((R * ROWS, TILES * T), BF16),
                 pltpu.VMEM((TILES * T, 2 * T), BF16),
                 pltpu.VMEM((2 * T, TILES * T), BF16),
-                pltpu.VMEM((R, ROWS + 2 * N, TILES * T), BF16),
+                pltpu.VMEM((R, ROWS + 2 * N, TILES * T), F32),
                 pltpu.VMEM((ROWS, 2 * T), F32),
                 pltpu.VMEM((4 * N, 2 * T), F32),
                 pltpu.VMEM((4 * EDGE, 2 * T), F32),

time: 37.1 us -> 33.8 us (0.911)
  the two profiles are of different devices: /device:TPU:0 before, /device:TPU:38 now
where the time goes in v2:
time: 33.8 us; the launch traced here: 33.6 us
  Pallas kernels  33 us (98%)
  between operations  0.64 us (2%)
    pallas_call x1, Pallas kernels, local(): pl.pallas_call(functools.partial(kernel, nx, ny), out_shape=(out, out, ja...  30.1 us
    pallas_call x1, Pallas kernels, local(): pl.pallas_call(last, grid=(2,), out_shape=(out, out), in_specs=[half, hal...  2.86 us

profile of v2, /device:TPU:38, one launch (start us, length us, event | category | flops | bytes accessed | tf_op | source)
XLA Modules:
  0.0 33.6 jit_solution(18672169509520550)
XLA Ops:
  0.6 30.1 %shard_map.95 = (bf16[1536,192]{1,0:T(8,128)(2,1)}, bf16[1536,192]{1,0:T(8,128)(2,1)}, f32[256,256]{1,0:T(8,128)}) custom-call(bf16[1536,192]{1,0:T(8,128)(2,1)} %bitcast.5, bf16[1536,192]{1,0:T(8,128)(2,1)} %bitcast.6, s32[16,16]{1,0:T(8,128)} %cls.1, s32[8,8]{1,0:T(8,128)} %slot.1, f32[64,192]{1,0:T(8,128)} %bitcast.7, f32[8,192]{1,0:T(8,128)} %adm.1, ...), custom_call_target="tpu_custom_call" | custom-call | tf_op jit(solution)/shard_map/pallas_call | solution.py:540
  30.7 2.9 %shard_map.96 = (bf16[1536,192]{1,0:T(8,128)(2,1)}, bf16[1536,192]{1,0:T(8,128)(2,1)}) custom-call(bf16[1536,192]{1,0:T(8,128)(2,1)} %get-tuple-element.7.rest, bf16[1536,192]{1,0:T(8,128)(2,1)} %get-tuple-element.8.back, f32[256,256]{1,0:T(8,128)} %get-tuple-element.9.admit, bf16[192,192]{1,0:T(8,128)(2,1)} %sinv.3), custom_call_target="tpu_custom_call" | custom-call | tf_op jit(solution)/shard_map/pallas_call | solution.py:589

commit v3 on v2

--- a/solution.py
+++ b/solution.py
@@ -488,8 +488,8 @@
     edges_a(0)
     pl.semaphore_wait(barrier, 8)
     start(0, 0)
+    main_f()
     start(1, 0)
-    main_f()
 
     def sweep(v, carry):
         main_a()
@@ -509,11 +509,19 @@
     main_a()
     arrive(0, SWEEPS - 1)
     correct_f(SWEEPS - 1)
-    inc[...] = right_f()
+    step = 2 * N
+    for k in range(MANY // step):
+        at = slice(k * step, (k + 1) * step)
+        near = jnp.concatenate([near_a[at, :], near_h[at, 0:HALF]], axis=1)
+        inc[at, :] = (inc[at, :].astype(F32) - near).astype(BF16)
     stores[0].start()
     arrive(1, SWEEPS - 1)
     correct_a(SWEEPS - 1)
-    src[...] = right_a()
+    for k in range(MANY // step):
+        at = slice(k * step, (k + 1) * step)
+        scale = admit[(k * step) % ROWS:(k * step) % ROWS + step, 0:U]
+        far = jnp.concatenate([far_a[at, :], far_h[at, 0:HALF]], axis=1)
+        src[at, :] = ((src[at, :].astype(F32) - far) * scale).astype(BF16)
     stores[1].start()
     for kind in range(2):
         for v in range(SWEEPS):

time: 33.8 us -> 33.1 us (0.979)
  the two profiles are of different devices: /device:TPU:38 before, /device:TPU:6 now
where the time goes in v3:
time: 33.1 us; the launch traced here: 33 us
  Pallas kernels  32.3 us (98%)
  between operations  0.64 us (2%)
    pallas_call x1, Pallas kernels, local(): pl.pallas_call(functools.partial(kernel, nx, ny), out_shape=(out, out, ja...  29.5 us
    pallas_call x1, Pallas kernels, local(): pl.pallas_call(last, grid=(2,), out_shape=(out, out), in_specs=[half, hal...  2.85 us

profile of v3, /device:TPU:6, one launch (start us, length us, event | category | flops | bytes accessed | tf_op | source)
XLA Modules:
  0.0 33.0 jit_solution(5663974515342229229)
XLA Ops:
  0.6 29.5 %shard_map.95 = (bf16[1536,192]{1,0:T(8,128)(2,1)}, bf16[1536,192]{1,0:T(8,128)(2,1)}, f32[256,256]{1,0:T(8,128)}) custom-call(bf16[1536,192]{1,0:T(8,128)(2,1)} %bitcast.5, bf16[1536,192]{1,0:T(8,128)(2,1)} %bitcast.6, s32[16,16]{1,0:T(8,128)} %cls.1, s32[8,8]{1,0:T(8,128)} %slot.1, f32[64,192]{1,0:T(8,128)} %bitcast.7, f32[8,192]{1,0:T(8,128)} %adm.1, ...), custom_call_target="tpu_custom_call" | custom-call | tf_op jit(solution)/shard_map/pallas_call | solution.py:548
  30.1 2.9 %shard_map.96 = (bf16[1536,192]{1,0:T(8,128)(2,1)}, bf16[1536,192]{1,0:T(8,128)(2,1)}) custom-call(bf16[1536,192]{1,0:T(8,128)(2,1)} %get-tuple-element.7.rest, bf16[1536,192]{1,0:T(8,128)(2,1)} %get-tuple-element.8.back, f32[256,256]{1,0:T(8,128)} %get-tuple-element.9.admit, bf16[192,192]{1,0:T(8,128)(2,1)} %sinv.3), custom_call_target="tpu_custom_call" | custom-call | tf_op jit(solution)/shard_map/pallas_call | solution.py:597
